TPU v7x, 512 devices: a whole 4x8x8 slice. The times are simulated.
512 devices in a mesh: ctx: 16 (over y, core), ch: 32 (over z, x).
Axes of the slice: x: 4, y: 8, z: 8, core: 2. Of those that a mesh axis runs over, the one named last changes fastest.
Arguments:
- records: bfloat16 [8192, 3, 4096], P(('ctx', 'ch')), may hold values from -6 to 6
- rec_slot: int32 [16, 32], replicated, may hold values from 0 to 31, as said below
- short_w: float32 [3, 4096, 3], P(None, 'ch'), may hold values from -3 to 3
- residue: float32 [4096, 16], P('ch'), may hold values from -5 to 5
- rate: float32 [4096, 16], P('ch'), may hold values from 6.1035156e-05 to 0.03
- passthrough: float32 [4096], P('ch'), may hold values from -4 to 4
Outputs:
- gated_out: bfloat16 [8192, 4096], P('ctx', 'ch')
Inputs may be any that keep to these rules, and one draw needn't show every extreme that they name: Record r entering along ctx index s goes to ctx index r mod 16; there rec_slot[s, r] is its record slot, and the records reaching one index take each slot 0 to 31 exactly once.
All inputs are finite; a program needn't handle non-finite values.
Results may differ from a plain program's by a relative error of at most 0.008.
Values may be sent and summed in bfloat16 or wider, within the bound.
A program may use at most 64 MiB of HBM per device.

v0:
```python
import math

import jax
import jax.numpy as jnp
from jax import lax
from jax.sharding import PartitionSpec as P

DFT_BLOCK = 64


PRECISE = lax.Precision.HIGHEST
FULL_TURN = 2.0 * math.pi


def from_behind(value, axis, steps):
    count = lax.axis_size(axis)
    leading, last = (max(0, -steps), min(count, count - steps))
    return lax.ppermute(value, axis, [(source, source + steps) for source in range(leading, last)])


def angle_table(left_idx, right_idx, period):
    products = left_idx[:, None] * right_idx[None, :] % period
    angles = products.astype(jnp.float32) * (FULL_TURN / period)
    return (jnp.cos(angles), jnp.sin(angles))


def steps_of(length):
    return jnp.arange(length, dtype=jnp.int32)


def across_forward(pieces):
    group_count = pieces.shape[0]
    cos_tab, sine_tab = angle_table(
        steps_of(2 * group_count), steps_of(group_count), 2 * group_count
    )
    real_part = jnp.einsum("kp,prc->krc", cos_tab, pieces, precision=PRECISE)
    imag_part = -jnp.einsum("kp,prc->krc", sine_tab, pieces, precision=PRECISE)
    return jnp.stack([real_part, imag_part])


def across_inverse(spectra, full_len):
    group_count = spectra.shape[1] // 2
    cos_tab, sine_tab = angle_table(
        steps_of(group_count), steps_of(2 * group_count), 2 * group_count
    )
    summed = jnp.einsum("pk,krc->prc", cos_tab, spectra[0], precision=PRECISE) - jnp.einsum(
        "pk,krc->prc", sine_tab, spectra[1], precision=PRECISE
    )
    return summed / full_len


def local_forward(spectra, freq_rows, full_len, radix_one):
    length = spectra.shape[2]
    radix_two = length // radix_one
    cos_tab, sine_tab = angle_table(freq_rows, steps_of(length), full_len)
    cos_tab = cos_tab[:, :, None]
    sine_tab = sine_tab[:, :, None]
    real_a = spectra[0] * cos_tab + spectra[1] * sine_tab
    imag_a = spectra[1] * cos_tab - spectra[0] * sine_tab
    grid_shape = (freq_rows.shape[0], radix_one, radix_two, spectra.shape[3])
    real_a = real_a.reshape(grid_shape)
    imag_a = imag_a.reshape(grid_shape)
    cos_one, sine_one = angle_table(steps_of(radix_one), steps_of(radix_one), radix_one)
    real_b = jnp.einsum("an,knbc->kabc", cos_one, real_a, precision=PRECISE) + jnp.einsum(
        "an,knbc->kabc", sine_one, imag_a, precision=PRECISE
    )
    imag_b = jnp.einsum("an,knbc->kabc", cos_one, imag_a, precision=PRECISE) - jnp.einsum(
        "an,knbc->kabc", sine_one, real_a, precision=PRECISE
    )
    cos_mid, sine_mid = angle_table(steps_of(radix_one), steps_of(radix_two), length)
    cos_mid = cos_mid[None, :, :, None]
    sine_mid = sine_mid[None, :, :, None]
    real_c = real_b * cos_mid + imag_b * sine_mid
    imag_c = imag_b * cos_mid - real_b * sine_mid
    cos_two, sine_two = angle_table(steps_of(radix_two), steps_of(radix_two), radix_two)
    real_d = jnp.einsum("bn,kanc->kabc", cos_two, real_c, precision=PRECISE) + jnp.einsum(
        "bn,kanc->kabc", sine_two, imag_c, precision=PRECISE
    )
    imag_d = jnp.einsum("bn,kanc->kabc", cos_two, imag_c, precision=PRECISE) - jnp.einsum(
        "bn,kanc->kabc", sine_two, real_c, precision=PRECISE
    )
    return (real_d, imag_d)


def local_inverse(real_a, imag_a, freq_rows, full_len):
    row_count, radix_one, radix_two, chan_width = real_a.shape
    length = radix_one * radix_two
    cos_two, sine_two = angle_table(steps_of(radix_two), steps_of(radix_two), radix_two)
    real_b = jnp.einsum("bn,kabc->kanc", cos_two, real_a, precision=PRECISE) - jnp.einsum(
        "bn,kabc->kanc", sine_two, imag_a, precision=PRECISE
    )
    imag_b = jnp.einsum("bn,kabc->kanc", cos_two, imag_a, precision=PRECISE) + jnp.einsum(
        "bn,kabc->kanc", sine_two, real_a, precision=PRECISE
    )
    cos_mid, sine_mid = angle_table(steps_of(radix_one), steps_of(radix_two), length)
    cos_mid = cos_mid[None, :, :, None]
    sine_mid = sine_mid[None, :, :, None]
    real_c = real_b * cos_mid - imag_b * sine_mid
    imag_c = imag_b * cos_mid + real_b * sine_mid
    cos_one, sine_one = angle_table(steps_of(radix_one), steps_of(radix_one), radix_one)
    real_d = jnp.einsum("am,kanc->kmnc", cos_one, real_c, precision=PRECISE) - jnp.einsum(
        "am,kanc->kmnc", sine_one, imag_c, precision=PRECISE
    )
    imag_d = jnp.einsum("am,kanc->kmnc", cos_one, imag_c, precision=PRECISE) + jnp.einsum(
        "am,kanc->kmnc", sine_one, real_c, precision=PRECISE
    )
    real_d = real_d.reshape(row_count, length, chan_width)
    imag_d = imag_d.reshape(row_count, length, chan_width)
    cos_tab, sine_tab = angle_table(freq_rows, steps_of(length), full_len)
    cos_tab = cos_tab[:, :, None]
    sine_tab = sine_tab[:, :, None]
    return jnp.stack([real_d * cos_tab - imag_d * sine_tab, imag_d * cos_tab + real_d * sine_tab])


def filter_spectrum(freq_rows, rate_part, resid_part, full_len, radix_one, radix_two):
    stride = full_len // (radix_one * radix_two)
    seq_total = full_len // 2
    mode_count = rate_part.shape[1]
    freq_index = freq_rows[:, None, None] + stride * (
        steps_of(radix_one)[None, :, None] + radix_one * steps_of(radix_two)[None, None, :]
    )
    centered = jnp.where(freq_index > full_len // 2, freq_index - full_len, freq_index)
    angles = (centered.astype(jnp.float32) * (FULL_TURN / full_len))[..., None]
    parity = (1 - 2 * (freq_index % 2)).astype(jnp.float32)[..., None]
    half_sin = jnp.sin(0.5 * angles)
    full_sin = jnp.sin(angles)

    def add_mode(mode_idx, carry):
        filt_real, filt_imag = carry
        rate_col = lax.dynamic_index_in_dim(rate_part, mode_idx, 1, keepdims=False)
        resid_col = lax.dynamic_index_in_dim(resid_part, mode_idx, 1, keepdims=False)
        coef_col = resid_col * jnp.sqrt(2.0 * rate_col / mode_count)
        decay_step = jnp.exp(-rate_col)
        decay_full = jnp.exp(-rate_col * seq_total)
        numer_part = 1.0 - parity * decay_full
        den_real = -jnp.expm1(-rate_col) + 2.0 * decay_step * half_sin * half_sin
        den_imag = decay_step * full_sin
        factor = coef_col * numer_part / (den_real * den_real + den_imag * den_imag)
        return (filt_real + factor * den_real, filt_imag - factor * den_imag)

    grid_shape = (freq_rows.shape[0], radix_one, radix_two, rate_part.shape[0])
    start = (jnp.zeros(grid_shape, jnp.float32), jnp.zeros(grid_shape, jnp.float32))
    return lax.fori_loop(0, mode_count, add_mode, start)


def filtered(spectra, freq_rows, rate_part, resid_part, full_len):
    radix_one = DFT_BLOCK
    radix_two = spectra.shape[2] // radix_one
    real_a, imag_a = local_forward(spectra, freq_rows, full_len, radix_one)
    filt_real, filt_imag = filter_spectrum(
        freq_rows, rate_part, resid_part, full_len, radix_one, radix_two
    )
    real_b = real_a * filt_real - imag_a * filt_imag
    imag_b = real_a * filt_imag + imag_a * filt_real
    return local_inverse(real_b, imag_b, freq_rows, full_len)


def shards(records, rec_slot, short_w, residue, rate, passthrough):
    ctx_count = lax.axis_size("ctx")
    ctx_index = lax.axis_index("ctx")
    streams = lax.all_to_all(records, "ch", split_axis=2, concat_axis=0, tiled=True)
    seq_rows, _, chan_width = streams.shape
    recs_all = rec_slot.shape[1]
    block_len = seq_rows // recs_all
    per_group = recs_all // ctx_count
    grouped = streams.reshape(per_group, ctx_count, block_len, 3, chan_width)
    arrived = lax.all_to_all(grouped, "ctx", split_axis=1, concat_axis=1, tiled=True)
    slot_list = lax.dynamic_index_in_dim(
        rec_slot.reshape(ctx_count, per_group, ctx_count), ctx_index, 2, keepdims=False
    )
    slot_list = slot_list.T.reshape(recs_all)
    selector = (steps_of(recs_all)[:, None] == slot_list[None, :]).astype(jnp.bfloat16)
    placed = jnp.dot(
        selector,
        arrived.reshape(recs_all, block_len * 3 * chan_width),
        preferred_element_type=jnp.float32,
    )
    placed = placed.astype(jnp.bfloat16).reshape(seq_rows, 3, chan_width)
    rim_rows = from_behind(placed[seq_rows - 2 :], "ctx", 1)
    extended = jnp.concatenate([rim_rows, placed], 0)
    features = (
        short_w[:, :, 0] * extended[2:]
        + short_w[:, :, 1] * extended[1:-1]
        + short_w[:, :, 2] * extended[:-2]
    )
    query_gate = features[:, 0, :]
    product = features[:, 1, :] * features[:, 2, :]
    full_len = 2 * seq_rows * ctx_count
    pieces = lax.all_to_all(product[None], "ctx", split_axis=1, concat_axis=0, tiled=True)
    spectra = across_forward(pieces)
    spectra = lax.all_to_all(spectra, "ctx", split_axis=1, concat_axis=2, tiled=True)
    freq_rows = ctx_index * 2 + steps_of(2)
    signals = filtered(spectra, freq_rows, rate, residue, full_len)
    signals = lax.all_to_all(
        signals.astype(jnp.bfloat16), "ctx", split_axis=2, concat_axis=1, tiled=True
    ).astype(signals.dtype)
    pieces = across_inverse(signals, full_len)
    convolved = lax.all_to_all(pieces, "ctx", split_axis=0, concat_axis=1, tiled=True)[0]
    return (query_gate * (convolved + passthrough * product)).astype(jnp.bfloat16)


def solution(mesh):
    return jax.shard_map(
        shards,
        mesh=mesh,
        in_specs=(
            P(("ctx", "ch"), None, None),
            P(),
            P(None, "ch", None),
            P("ch", None),
            P("ch", None),
            P("ch"),
        ),
        out_specs=P("ctx", "ch"),
        check_vma=False,
    )
```

profile of v0, /device:TPU:1, one launch (start us, length us, event | category | flops | bytes accessed | tf_op | source)
XLA Modules:
  0.0 195.2 jit_solution(1773822105562222145)
XLA Ops:
  0.0 5.7 %copy.184 = bf16[16,3,4096]{0,1,2:T(4,128)(2,1)} copy(bf16[16,3,4096]{2,0,1:T(8,128)(2,1)} %param.8) | data formatting | bytes 786432 | tf_op args[0]
  5.7 6.7 %reshape.422 = bf16[32,2,3072]{2,1,0:T(2,128)(2,1)S(1)} reshape(bf16[4096,3,16]{2,1,0:T(4,128)(2,1)} %bitcast.183) | data formatting | bytes 786432
  12.4 27.3 %all_to_all.71 = bf16[32,2,3072]{2,1,0:T(2,128)(2,1)S(1)} all-to-all(bf16[32,2,3072]{2,1,0:T(2,128)(2,1)S(1)} %reshape.422), channel_id=1, replica_groups=mesh['ctx'=16,'ch'=32] {'ch'}, dimensions={0} | all-to-all | bytes 786432 | tf_op jit(solution)/shard_map/all_to_all | solution.py:161
  39.7 5.6 %reshape.423 = bf16[4096,3,16]{2,1,0:T(4,128)(2,1)} reshape(bf16[32,2,3072]{2,1,0:T(2,128)(2,1)S(1)} %all_to_all.71) | data formatting | bytes 786432
  45.3 5.2 %copy.241 = bf16[16,3,32,128]{3,0,1,2:T(8,128)(2,1)S(1)} copy(bf16[16,3,32,128]{0,1,3,2:T(4,128)(2,1)} %bitcast.182) | data formatting | bytes 786432 | tf_op jit(solution)/shard_map/all_to_all | solution.py:161
  51.3 9.6 %all-to-all-start.1 = ((bf16[2,16,16,3,128]{4,2,3,0,1:T(8,128)(2,1)}), bf16[2,16,16,3,128]{4,2,3,0,1:T(8,128)(2,1)S(1)}, u32[]{:S(2)}, u32[]{:S(2)}) async-start(bf16[2,16,16,3,128]{4,2,3,0,1:T(8,128)(2,1)} %copy.187), calls=%async_computation.1 | async-start | bytes 786432 | tf_op jit(solution)/shard_map/all_to_all | solution.py:167
  61.3 14.2 %all-to-all-done.1 = bf16[2,16,16,3,128]{4,2,3,0,1:T(8,128)(2,1)S(1)} async-done(((bf16[2,16,16,3,128]{4,2,3,0,1:T(8,128)(2,1)}), bf16[2,16,16,3,128]{4,2,3,0,1:T(8,128)(2,1)S(1)}, u32[]{:S(2)}, u32[]{:S(2)}) %all-to-all-start.1) | async-done | bytes 393248 | tf_op jit(solution)/shard_map/all_to_all | solution.py:167
  76.9 1.9 collective-permute-start
  78.9 1.1 collective-permute-done
  80.7 1.2 slice_multiply_fusion
  81.9 5.9 %all-to-all-start.2 = ((f32[1,512,128]{2,0,1:T(1,128)}), f32[1,512,128]{2,0,1:T(1,128)S(1)}, u32[]{:S(2)}, u32[]{:S(2)}) async-start(f32[1,512,128]{2,0,1:T(1,128)} %bitcast.10), calls=%async_computation.2 | async-start | bytes 524288 | tf_op jit(solution)/shard_map/all_to_all | solution.py:189
  87.8 11.7 %all-to-all-done.2 = f32[1,512,128]{2,0,1:T(1,128)S(1)} async-done(((f32[1,512,128]{2,0,1:T(1,128)}), f32[1,512,128]{2,0,1:T(1,128)S(1)}, u32[]{:S(2)}, u32[]{:S(2)}) %all-to-all-start.2) | async-done | bytes 262176 | tf_op jit(solution)/shard_map/all_to_all | solution.py:189
  101.0 1.6 copy.193
  102.7 3.5 %all-to-all-start.3 = ((f32[2,32,32,128]{3,2,0,1:T(8,128)}), f32[2,32,32,128]{3,2,0,1:T(8,128)S(1)}, u32[]{:S(2)}, u32[]{:S(2)}) async-start(f32[2,32,32,128]{3,2,0,1:T(8,128)} %copy.193), calls=%async_computation.3 | async-start | bytes 2097152 | tf_op jit(solution)/shard_map/all_to_all | solution.py:191
  106.2 32.1 %while.20 = (s32[]{:T(128)}, f32[2,64,8,128]{3,2,1,0:T(8,128)S(1)}, f32[2,64,8,128]{3,2,1,0:T(8,128)S(1)}, f32[128,16]{0,1:T(8,128)}, f32[128,16]{0,1:T(8,128)},...) while((s32[]{:T(128)}, f32[2,64,8,128]{3,2,1,0:T(8,128)S(1)}, ...), condition=%wide.region_1.2_spmd.clone.clone.clone, body=%wide.region_0.1_spmd.clone.clone.clone.sunk | while | flops 2251523 | bytes 2133635 | solution.py:143
  141.9 0.9 multiply_add_fusion.3
  142.9 0.9 fusion.44
  143.8 0.9 fusion.40
  144.7 0.9 fusion.26
  145.7 1.1 multiply_add_fusion.2
  150.8 1.0 fusion.23
  153.9 23.8 %all_to_all.72 = bf16[2,2,512,128]{3,1,0,2:T(2,128)(2,1)S(1)} all-to-all(bf16[2,2,512,128]{3,1,0,2:T(2,128)(2,1)S(1)} %copy.223), channel_id=1, replica_groups=mesh['ctx'=16,'ch'=32] {'ctx'}, dimensions={2} | all-to-all | bytes 1048576 | tf_op jit(solution)/shard_map/all_to_all | solution.py:194
  179.1 14.4 %all_to_all.73 = f32[16,32,128]{2,1,0:T(8,128)S(1)} all-to-all(f32[16,32,128]{2,1,0:T(8,128)S(1)} %copy.227), channel_id=1, replica_groups=mesh['ctx'=16,'ch'=32] {'ctx'}, dimensions={0} | all-to-all | bytes 524288 | tf_op jit(solution)/shard_map/all_to_all | solution.py:198
  193.5 1.7 fusion.53
  (160 shorter events, 46.9 us)
Async XLA Ops:
  45.3 15.6 %copy-start = (s32[16,32]{1,0:T(8,128)S(1)}, s32[16,32]{1,0:T(8,128)}, u32[]{:S(2)}) copy-start(s32[16,32]{1,0:T(8,128)} %param.9) | copy-start | bytes 6148
  45.3 16.0 %copy-start.1 = (f32[3,128,3]{1,2,0:T(4,128)S(1)}, f32[3,128,3]{1,2,0:T(4,128)}, u32[]{:S(2)}) copy-start(f32[3,128,3]{1,2,0:T(4,128)} %param.10) | copy-start | bytes 13828
  51.3 24.2 %all-to-all-start.1 = ((bf16[2,16,16,3,128]{4,2,3,0,1:T(8,128)(2,1)}), bf16[2,16,16,3,128]{4,2,3,0,1:T(8,128)(2,1)S(1)}, u32[]{:S(2)}, u32[]{:S(2)}) async-start(bf16[2,16,16,3,128]{4,2,3,0,1:T(8,128)(2,1)} %copy.187), calls=%async_computation.1 | async-start | bytes 786432 | tf_op jit(solution)/shard_map/all_to_all | solution.py:167
  76.9 3.1 %collective-permute-start = (bf16[2,3,128]{2,1,0:T(4,128)(2,1)S(1)}, bf16[2,3,128]{2,1,0:T(4,128)(2,1)S(1)}, u32[]{:S(2)}, u32[]{:S(2)}) collective-permute-start(bf16[2,3,128]{2,1,0:T(4,128)(2,1)S(1)} %slice.58), channel_id=1, source_target_pairs={{0,32},{32,64},{64,96},{96,128},{128,160},{160,192},{192,224},{224... | collective-permute-start | bytes 4616 | tf_op jit(solution)/shard_map/ppermute | solution.py:18
  81.9 17.6 %all-to-all-start.2 = ((f32[1,512,128]{2,0,1:T(1,128)}), f32[1,512,128]{2,0,1:T(1,128)S(1)}, u32[]{:S(2)}, u32[]{:S(2)}) async-start(f32[1,512,128]{2,0,1:T(1,128)} %bitcast.10), calls=%async_computation.2 | async-start | bytes 524288 | tf_op jit(solution)/shard_map/all_to_all | solution.py:189
  102.7 36.3 %all-to-all-start.3 = ((f32[2,32,32,128]{3,2,0,1:T(8,128)}), f32[2,32,32,128]{3,2,0,1:T(8,128)S(1)}, u32[]{:S(2)}, u32[]{:S(2)}) async-start(f32[2,32,32,128]{3,2,0,1:T(8,128)} %copy.193), calls=%async_computation.3 | async-start | bytes 2097152 | tf_op jit(solution)/shard_map/all_to_all | solution.py:191
  153.3 40.3 %copy-start.2 = (f32[128]{0:T(128)S(1)}, f32[128]{0:T(128)}, u32[]{:S(2)}) copy-start(f32[128]{0:T(128)} %param.13) | copy-start | bytes 1540
where the time goes:
time: 197 us; the launch traced here: 195 us
  blocking collectives  65.6 us (33%)
  other arithmetic  35.9 us (18%)
  local copies, waits for them, and re-layouts  29.2 us (15%)
  waiting for transfers between devices  26.9 us (14%)
  starting transfers between devices  21 us (11%)
  matrix products  15.1 us (8%)
    all_to_all x1, blocking collectives, shards(): lax.all_to_all(records, 'ch', split_axis=2, concat_axis=0, tiled=True)  27.3 us
    all_to_all x1, blocking collectives, shards(): lax.all_to_all(signals.astype(jnp.bfloat16), 'ctx', split_axis=2, concat_...  23.8 us
    unnamed x13, local copies, waits for them, and re-layouts  18.1 us
    all_to_all x1, blocking collectives, shards(): lax.all_to_all(pieces, 'ctx', split_axis=0, concat_axis=1, tiled=True)[0]  14.4 us
    all_to_all x1, waiting for transfers between devices, shards(): lax.all_to_all(grouped, 'ctx', split_axis=1, concat_axis=1, tiled=True)  14.2 us
    all_to_all x1, waiting for transfers between devices, shards(): lax.all_to_all(product[None], 'ctx', split_axis=1, concat_axis=0, tiled=T...  11.7 us
    exp x16, other arithmetic, add_mode(): decay_full = jnp.exp(-rate_col * seq_total)  11.6 us
    all_to_all x1, starting transfers between devices, shards(): lax.all_to_all(grouped, 'ctx', split_axis=1, concat_axis=1, tiled=True)  9.61 us
  transfers between devices with their start and end apart: 4, of which 3 were waited for; matrix products, arithmetic and copies ran while one was open for 16% of the time, Pallas kernels for 0%

commit v1 on v0

v1 whole, which is shorter than its diff:
```python
import functools
import math

import jax
import jax.numpy as jnp
from jax import lax
from jax.experimental import pallas as pl
from jax.experimental.pallas import tpu as pltpu
from jax.sharding import PartitionSpec as P

MESH = pl.DeviceIdType.MESH
LANES = 128
CHUNKS = 8
STRIDE = 13
MESSAGE = 32


def kernel(
    n_ctx,
    n_ch,
    block,
    modes,
    x_ref,
    slot_ref,
    w_ref,
    res_ref,
    rate_ref,
    pass_ref,
    out_ref,
    abuf,
    bbuf,
    perm,
    placed,
    pbuf,
    qbuf,
    ybuf,
    tail,
    local,
    met,
    send_a,
    recv_a,
    send_b,
    recv_b,
    send_c,
    recv_c,
):
    s = lax.axis_index("ctx")
    c = lax.axis_index("ch")
    recs = n_ch
    group = recs // n_ctx
    seq = recs * block
    steps = seq // CHUNKS
    f32 = jnp.float32

    barrier = pltpu.get_barrier_semaphore()

    @pl.loop(1, n_ch)
    def _(k):
        pl.semaphore_signal(
            barrier, inc=1, device_id={"ch": lax.rem(c + k, n_ch)}, device_id_type=MESH
        )

    @pl.loop(1, n_ctx)
    def _(k):
        pl.semaphore_signal(
            barrier, inc=1, device_id={"ctx": lax.rem(s + k, n_ctx)}, device_id_type=MESH
        )

    pl.semaphore_wait(barrier, n_ch + n_ctx - 2)

    def block_of(ch):
        return x_ref.at[:, :, pl.ds(pl.multiple_of(ch * LANES, LANES), LANES)]

    def copy_a(ch):
        return pltpu.make_async_remote_copy(
            src_ref=block_of(ch),
            dst_ref=abuf.at[c],
            send_sem=send_a.at[ch],
            recv_sem=recv_a.at[c],
            device_id={"ch": ch},
            device_id_type=MESH,
        )

    def offset(k):
        return lax.rem(STRIDE * (k + s), n_ch)

    @pl.loop(0, n_ch)
    def _(k):
        ch = lax.rem(c + offset(k), n_ch)

        @pl.when(ch != c)
        def _():
            copy_a(ch).start()

        @pl.when(ch == c)
        def _():
            pltpu.make_async_copy(block_of(c), abuf.at[c], recv_a.at[c]).start()

    col = lax.broadcasted_iota(jnp.int32, (recs, seq), 1)
    row = lax.broadcasted_iota(jnp.int32, (recs, seq), 0)
    pick = (row == (col // block) % group * n_ctx + s).astype(f32)
    spread = jnp.dot(slot_ref[...].astype(f32), pick, preferred_element_type=f32)
    col = lax.broadcasted_iota(jnp.int32, (n_ctx, seq), 1)
    row = lax.broadcasted_iota(jnp.int32, (n_ctx, seq), 0)
    spread = jnp.where(row == col // (block * group), spread, 0.0)
    target = jnp.sum(spread, axis=0, keepdims=True).astype(jnp.int32)
    target = target * block + lax.broadcasted_iota(jnp.int32, (1, seq), 1) % block
    target = target % steps * CHUNKS + target // steps

    rows_at_once = 16

    @pl.loop(0, seq // rows_at_once)
    def _(i):
        at = pl.multiple_of(i * rows_at_once, rows_at_once)
        here = lax.broadcasted_iota(jnp.int32, (rows_at_once, seq), 0) + at
        perm[pl.ds(at, rows_at_once), :] = jnp.where(here == target, 1.0, 0.0).astype(jnp.bfloat16)

    @pl.loop(s + 2, n_ctx + 1)
    def _(i):
        met[pl.ds(pl.multiple_of(i * MESSAGE, MESSAGE), MESSAGE), :] = jnp.zeros((MESSAGE, LANES), f32)

    met[0:MESSAGE, :] = jnp.zeros((MESSAGE, LANES), f32)

    def landing(source, half):
        return bbuf.at[source * group + half]

    def copy_b(r):
        return pltpu.make_async_remote_copy(
            src_ref=abuf.at[r],
            dst_ref=landing(s, r // n_ctx),
            send_sem=send_b.at[r],
            recv_sem=recv_b.at[s * group + r // n_ctx],
            device_id={"ctx": lax.rem(r, n_ctx)},
            device_id_type=MESH,
        )

    @pl.loop(0, n_ch)
    def _(k):
        r = lax.rem(c + n_ch - offset(k), n_ch)
        pltpu.make_async_copy(abuf.at[r], abuf.at[r], recv_a.at[r]).wait()
        owner = lax.rem(r, n_ctx)

        @pl.when(owner != s)
        def _():
            copy_b(r).start()

        @pl.when(owner == s)
        def _():
            i = s * group + r // n_ctx
            pltpu.make_async_copy(abuf.at[r], bbuf.at[i], recv_b.at[i]).start()

    rate = rate_ref[...]
    decay = jnp.exp(-rate)
    gain = res_ref[...] * jnp.sqrt(2.0 * rate / modes)
    chunk_id = lax.broadcasted_iota(jnp.int32, (CHUNKS, LANES), 0)

    def spread_row(table, m):
        return jnp.broadcast_to(table[m : m + 1, :], (CHUNKS, LANES))

    @pl.loop(0, n_ch)
    def _(i):
        pltpu.make_async_copy(bbuf.at[i], bbuf.at[i], recv_b.at[i]).wait()

    for j in range(3):
        placed[j] = jnp.dot(
            perm[...], bbuf[:, j].reshape(seq, LANES), preferred_element_type=f32
        )

    taps = [[jnp.broadcast_to(w_ref[j, i : i + 1, :], (CHUNKS, LANES)) for i in range(3)] for j in range(3)]
    decays = [spread_row(decay, m) for m in range(modes)]
    before = [
        [
            jnp.where(chunk_id == 0, 0.0, pltpu.roll(placed[j, (steps - i) * CHUNKS : (steps - i + 1) * CHUNKS, :], 1, 0))
            for j in range(3)
        ]
        for i in (1, 2)
    ]

    def first_pass(t, carry):
        one, two, state = carry
        at = pl.ds(pl.multiple_of(t * CHUNKS, CHUNKS), CHUNKS)
        now = [placed[j, at, :] for j in range(3)]
        feats = [taps[j][0] * now[j] + taps[j][1] * one[j] + taps[j][2] * two[j] for j in range(3)]
        product = feats[1] * feats[2]
        if isinstance(t, int):
            product = jnp.where(chunk_id == 0, 0.0, product)
        qbuf[at, :] = feats[0]
        pbuf[at, :] = product
        state = [decays[m] * state[m] + product for m in range(modes)]
        return now, one, state

    carry = (before[0], before[1], [jnp.zeros((CHUNKS, LANES), f32)] * modes)
    carry = first_pass(0, carry)
    carry = first_pass(1, carry)
    _, _, state = lax.fori_loop(2, steps, first_pass, carry, unroll=2)

    start = []
    for m in range(modes):
        total = state[m]
        for hop in (1, 2, 4):
            power = spread_row(jnp.exp(-rate[m : m + 1, :] * (steps * hop)), 0)
            total = total + power * jnp.where(chunk_id >= hop, pltpu.roll(total, hop, 0), 0.0)
        local[m : m + 1, :] = total[CHUNKS - 1 :, :]
        start.append(jnp.where(chunk_id >= 1, pltpu.roll(total, 1, 0), 0.0))
    for j in range(3):
        for i in range(2):
            local[modes + 2 * j + i : modes + 2 * j + i + 1, :] = placed[j, i * CHUNKS : i * CHUNKS + 1, :]
            at = (steps - 2 + i) * CHUNKS + CHUNKS - 1
            local[modes + 6 + 2 * j + i : modes + 7 + 2 * j + i, :] = placed[j, at : at + 1, :]
    local[modes + 12 :, :] = jnp.zeros((MESSAGE - modes - 12, LANES), f32)

    def slab(shard):
        return met.at[pl.ds(pl.multiple_of((shard + 1) * MESSAGE, MESSAGE), MESSAGE)]

    def copy_c(shard):
        return pltpu.make_async_remote_copy(
            src_ref=local,
            dst_ref=slab(s),
            send_sem=send_c.at[shard],
            recv_sem=recv_c.at[s],
            device_id={"ctx": shard},
            device_id_type=MESH,
        )

    @pl.loop(s + 1, n_ctx)
    def _(shard):
        copy_c(shard).start()

    met[pl.ds(pl.multiple_of((s + 1) * MESSAGE, MESSAGE), MESSAGE), :] = local[...]

    gains = [spread_row(gain, m) for m in range(modes)]

    def second_pass(t, state):
        at = pl.ds(pl.multiple_of(t * CHUNKS, CHUNKS), CHUNKS)
        product = pbuf[at, :]
        state = [decays[m] * state[m] + product for m in range(modes)]
        terms = [gains[m] * state[m] for m in range(modes)]
        while len(terms) > 1:
            terms = [a + b for a, b in zip(terms[::2], terms[1::2])]
        ybuf[at, :] = terms[0]
        return state

    lax.fori_loop(0, steps, second_pass, start, unroll=2)

    @pl.loop(0, s)
    def _(shard):
        pltpu.make_async_copy(slab(shard), slab(shard), recv_c.at[shard]).wait()

    def rim(row, width, base, stride):
        return met[pl.ds(base + row, width, stride=stride), :]

    def rim_products(pick_row):
        first, second = [], []
        for j in range(3):
            x0, x1 = pick_row(MESSAGE + modes + 2 * j), pick_row(MESSAGE + modes + 2 * j + 1)
            l0, l1 = pick_row(modes + 6 + 2 * j), pick_row(modes + 7 + 2 * j)
            tap = [w_ref[j, i : i + 1, :] for i in range(3)]
            first.append(tap[0] * x0 + tap[1] * l1 + tap[2] * l0)
            second.append(tap[0] * x1 + tap[1] * x0 + tap[2] * l1)
        return first[0], first[1] * first[2], second[0], second[1] * second[2]

    _, all0, _, all1 = rim_products(lambda i: met[pl.ds(i, n_ctx, stride=MESSAGE), :])
    here = met[pl.ds(pl.multiple_of(s * MESSAGE, MESSAGE), 2 * MESSAGE), :]
    q0, p0, q1, p1 = rim_products(lambda i: here[i : i + 1, :])

    back0 = jnp.exp(-rate * (seq - 1))
    back1 = jnp.exp(-rate * (seq - 2))
    entering = jnp.zeros((modes, LANES), f32)
    for shard in range(n_ctx - 1):
        behind = s - 1 - shard
        reach = jnp.exp(-rate * (seq * jnp.maximum(behind, 0)).astype(f32))
        reach = jnp.where(behind >= 0, reach, 0.0)
        ended = met[(shard + 1) * MESSAGE : (shard + 1) * MESSAGE + modes, :]
        ended = ended + back0 * all0[shard : shard + 1, :] + back1 * all1[shard : shard + 1, :]
        entering = entering + reach * ended
    grow = jnp.exp(rate)
    entering = entering + grow * (p0 + grow * p1)
    early = jnp.sum(gain * grow, axis=0, keepdims=True) * p1

    pbuf[0:1, :] = p0
    qbuf[0:1, :] = q0
    pbuf[CHUNKS : CHUNKS + 1, :] = p1
    qbuf[CHUNKS : CHUNKS + 1, :] = q1
    ybuf[0:1, :] = ybuf[0:1, :] - early

    since = (chunk_id * steps + 1).astype(f32)
    coming = [
        spread_row(gain * entering, m) * jnp.exp(-spread_row(rate, m) * since) for m in range(modes)
    ]
    direct = jnp.broadcast_to(pass_ref[...], (CHUNKS, LANES))

    def third_pass(t, coming):
        at = pl.ds(pl.multiple_of(t * CHUNKS, CHUNKS), CHUNKS)
        terms = coming
        while len(terms) > 1:
            terms = [a + b for a, b in zip(terms[::2], terms[1::2])]
        value = qbuf[at, :] * (ybuf[at, :] + terms[0] + direct * pbuf[at, :])
        tail[pl.ds(t, CHUNKS, stride=steps), :] = value
        return [decays[m] * coming[m] for m in range(modes)]

    lax.fori_loop(0, steps, third_pass, coming, unroll=2)
    out_ref[...] = tail[...].astype(out_ref.dtype)

    @pl.loop(1, n_ch)
    def _(k):
        copy_a(lax.rem(c + k, n_ch)).wait_send()

    @pl.loop(0, n_ch)
    def _(r):
        @pl.when(lax.rem(r, n_ctx) != s)
        def _():
            copy_b(r).wait_send()

    @pl.loop(s + 1, n_ctx)
    def _(shard):
        copy_c(shard).wait_send()


def shards(n_ctx, n_ch, records, rec_slot, short_w, residue, rate, passthrough):
    block, _, channels = records.shape
    modes = rate.shape[1]
    seq = n_ch * block
    f32 = jnp.float32
    vmem = pl.BlockSpec(memory_space=pltpu.VMEM)
    dma = pltpu.SemaphoreType.DMA
    return pl.pallas_call(
        functools.partial(kernel, n_ctx, n_ch, block, modes),
        out_shape=jax.ShapeDtypeStruct((seq, LANES), jnp.bfloat16),
        in_specs=[pl.BlockSpec(memory_space=pl.ANY)] + [vmem] * 5,
        out_specs=vmem,
        scratch_shapes=[
            pltpu.VMEM((n_ch, 3, block, LANES), jnp.bfloat16),
            pltpu.VMEM((n_ch, 3, block, LANES), jnp.bfloat16),
            pltpu.VMEM((seq, seq), jnp.bfloat16),
            pltpu.VMEM((3, seq, LANES), f32),
            pltpu.VMEM((seq, LANES), f32),
            pltpu.VMEM((seq, LANES), f32),
            pltpu.VMEM((seq, LANES), f32),
            pltpu.VMEM((seq, LANES), f32),
            pltpu.VMEM((MESSAGE, LANES), f32),
            pltpu.VMEM(((n_ctx + 1) * MESSAGE, LANES), f32),
            dma((n_ch,)),
            dma((n_ch,)),
            dma((n_ch,)),
            dma((n_ch,)),
            dma((n_ctx,)),
            dma((n_ctx,)),
        ],
        compiler_params=pltpu.CompilerParams(
            collective_id=0, has_side_effects=True, vmem_limit_bytes=48 * 1024 * 1024
        ),
        name="hyena",
    )(
        records.transpose(1, 0, 2),
        rec_slot,
        short_w.transpose(0, 2, 1),
        residue.T,
        rate.T,
        passthrough[None, :],
    )


def solution(mesh):
    return jax.shard_map(
        functools.partial(shards, mesh.shape["ctx"], mesh.shape["ch"]),
        mesh=mesh,
        in_specs=(
            P(("ctx", "ch"), None, None),
            P(),
            P(None, "ch", None),
            P("ch", None),
            P("ch", None),
            P("ch"),
        ),
        out_specs=P("ctx", "ch"),
        check_vma=False,
    )
```

time: 197 us -> 47.8 us (0.24)
  the two profiles are of different devices: /device:TPU:1 before, /device:TPU:48 now
where the time goes in v1:
time: 47.8 us; the launch traced here: 47.2 us
  Pallas kernels  42.8 us (90%)
  local copies, waits for them, and re-layouts  4.44 us (9%)
    pallas_call x1, Pallas kernels, shards(): pl.pallas_call(functools.partial(kernel, n_ctx, n_ch, block, modes), out_...  42.8 us
    unnamed x13, local copies, waits for them, and re-layouts  4.44 us

profile of v1, /device:TPU:48, one launch (start us, length us, event | category | flops | bytes accessed | tf_op | source)
XLA Modules:
  0.0 47.2 jit_solution(9550519525805510204)
XLA Ops:
  0.0 0.0 copy-start.1
  0.0 0.0 copy-start.5
  0.0 0.7 %copy-done.1 = s32[16,32]{1,0:T(8,128)S(1)} copy-done((s32[16,32]{1,0:T(8,128)S(1)}, s32[16,32]{1,0:T(8,128)}, u32[]{:S(2)}) %copy-start.1) | copy-done | bytes 2072
  0.7 0.0 copy-done.5
  0.7 0.0 copy-start
  0.7 1.0 %copy-done = bf16[16,3,4096]{2,0,1:T(8,128)(2,1)S(1)} copy-done((bf16[16,3,4096]{2,0,1:T(8,128)(2,1)S(1)}, bf16[16,3,4096]{2,0,1:T(8,128)(2,1)}, u32[]{:S(2)}) %copy-start) | copy-done | bytes 393240
  1.7 0.0 copy-start.2
  1.7 0.7 %copy-done.2 = f32[128,16]{0,1:T(8,128)S(1)} copy-done((f32[128,16]{0,1:T(8,128)S(1)}, f32[128,16]{0,1:T(8,128)}, u32[]{:S(2)}) %copy-start.2) | copy-done | bytes 8216
  2.4 0.0 copy-start.3
  2.4 0.7 %copy-done.3 = f32[128,16]{0,1:T(8,128)S(1)} copy-done((f32[128,16]{0,1:T(8,128)S(1)}, f32[128,16]{0,1:T(8,128)}, u32[]{:S(2)}) %copy-start.3) | copy-done | bytes 8216
  3.1 0.0 copy-start.4
  3.1 0.7 %copy-done.4 = f32[3,128,3]{1,2,0:T(4,128)S(1)} copy-done((f32[3,128,3]{1,2,0:T(4,128)S(1)}, f32[3,128,3]{1,2,0:T(4,128)}, u32[]{:S(2)}) %copy-start.4) | copy-done | bytes 4632
  3.8 42.8 %hyena.1 = bf16[512,128]{1,0:T(8,128)(2,1)S(1)} custom-call(bf16[3,16,4096]{2,1,0:T(8,128)(2,1)S(1)} %bitcast.5, s32[16,32]{1,0:T(8,128)S(1)} %copy-done.1, f32[3,3,128]{2,1,0:T(4,128)S(1)} %bitcast.8, f32[16,128]{1,0:T(8,128)S(1)} %bitcast.6, f32[16,128]{1,0:T(8,128)S(1)} %bitcast.7, f32[1,128]{1,0:T(1,128)S(1)} %bitcast.9), custom_call_target="tpu_custom_call" | custom-call | tf_op jit(solution)/shard_map/hyena/pallas_call | solution.py:326
  46.6 0.7 %copy.8 = bf16[512,128]{1,0:T(8,128)(2,1)} copy(bf16[512,128]{1,0:T(8,128)(2,1)S(1)} %hyena.1) | data formatting | bytes 262144
Async XLA Ops:
  0.0 0.7 %copy-start.1 = (s32[16,32]{1,0:T(8,128)S(1)}, s32[16,32]{1,0:T(8,128)}, u32[]{:S(2)}) copy-start(s32[16,32]{1,0:T(8,128)} %slot_ref.1) | copy-start | bytes 6148
  0.0 0.7 %copy-start.5 = (f32[128]{0:T(128)S(1)}, f32[128]{0:T(128)}, u32[]{:S(2)}) copy-start(f32[128]{0:T(128)} %param.11) | copy-start | bytes 1540
  0.7 1.0 %copy-start = (bf16[16,3,4096]{2,0,1:T(8,128)(2,1)S(1)}, bf16[16,3,4096]{2,0,1:T(8,128)(2,1)}, u32[]{:S(2)}) copy-start(bf16[16,3,4096]{2,0,1:T(8,128)(2,1)} %param.6) | copy-start | bytes 1179652
  1.7 0.7 %copy-start.2 = (f32[128,16]{0,1:T(8,128)S(1)}, f32[128,16]{0,1:T(8,128)}, u32[]{:S(2)}) copy-start(f32[128,16]{0,1:T(8,128)} %param.9) | copy-start | bytes 24580
  2.4 0.7 %copy-start.3 = (f32[128,16]{0,1:T(8,128)S(1)}, f32[128,16]{0,1:T(8,128)}, u32[]{:S(2)}) copy-start(f32[128,16]{0,1:T(8,128)} %param.10) | copy-start | bytes 24580
  3.1 0.7 %copy-start.4 = (f32[3,128,3]{1,2,0:T(4,128)S(1)}, f32[3,128,3]{1,2,0:T(4,128)}, u32[]{:S(2)}) copy-start(f32[3,128,3]{1,2,0:T(4,128)} %param.8) | copy-start | bytes 13828

commit v2 on v1

--- a/solution.py
+++ b/solution.py
@@ -1,5 +1,4 @@
 import functools
-import math
 
 import jax
 import jax.numpy as jnp
@@ -11,8 +10,13 @@
 MESH = pl.DeviceIdType.MESH
 LANES = 128
 CHUNKS = 8
-STRIDE = 13
+INNER = 4
+CORES = 2
 MESSAGE = 32
+
+
+def near_first(count):
+    return [(i + 1) // 2 if i % 2 else -(i // 2) for i in range(count)]
 
 
 def kernel(
@@ -20,13 +24,18 @@
     n_ch,
     block,
     modes,
-    x_ref,
+    x_hbm,
+    slot_hbm,
+    w_hbm,
+    res_hbm,
+    rate_hbm,
+    pass_hbm,
+    out_ref,
     slot_ref,
     w_ref,
     res_ref,
     rate_ref,
     pass_ref,
-    out_ref,
     abuf,
     bbuf,
     perm,
@@ -37,12 +46,17 @@
     tail,
     local,
     met,
+    tables,
+    starts,
+    load,
     send_a,
     recv_a,
     send_b,
     recv_b,
     send_c,
     recv_c,
+    ready_a,
+    ready_b,
 ):
     s = lax.axis_index("ctx")
     c = lax.axis_index("ch")
@@ -51,51 +65,71 @@
     seq = recs * block
     steps = seq // CHUNKS
     f32 = jnp.float32
+    n_z, n_y = n_ch // INNER, n_ctx // CORES
+
+    def place_of(ctx):
+        y = ctx // CORES
+        return jnp.where(y == 0, 0, jnp.where(y <= n_y // 2, 2 * y - 1, 2 * (n_y - y))) * CORES + ctx % CORES
+
+    def ctx_at(place):
+        i = place // CORES
+        return jnp.where(i == 0, 0, jnp.where(i % 2 == 1, (i + 1) // 2, n_y - i // 2)) * CORES + place % CORES
+
+    place = place_of(s)
+
+    operands = [(slot_hbm, slot_ref), (w_hbm, w_ref), (res_hbm, res_ref), (rate_hbm, rate_ref), (pass_hbm, pass_ref)]
+    fetches = [pltpu.make_async_copy(src, dst, load.at[i]) for i, (src, dst) in enumerate(operands)]
 
     barrier = pltpu.get_barrier_semaphore()
 
-    @pl.loop(1, n_ch)
-    def _(k):
-        pl.semaphore_signal(
-            barrier, inc=1, device_id={"ch": lax.rem(c + k, n_ch)}, device_id_type=MESH
-        )
-
-    @pl.loop(1, n_ctx)
-    def _(k):
-        pl.semaphore_signal(
-            barrier, inc=1, device_id={"ctx": lax.rem(s + k, n_ctx)}, device_id_type=MESH
-        )
-
-    pl.semaphore_wait(barrier, n_ch + n_ctx - 2)
+    @pl.loop(c + 1, n_ch)
+    def _(ch):
+        pl.semaphore_signal(barrier, inc=1, device_id={"ch": ch}, device_id_type=MESH)
+
+    @pl.loop(place + 1, n_ctx)
+    def _(p):
+        pl.semaphore_signal(barrier, inc=1, device_id={"ctx": ctx_at(p)}, device_id_type=MESH)
 
     def block_of(ch):
-        return x_ref.at[:, :, pl.ds(pl.multiple_of(ch * LANES, LANES), LANES)]
+        return x_hbm.at[:, :, pl.ds(pl.multiple_of(ch * LANES, LANES), LANES)]
+
+    pltpu.make_async_copy(block_of(c), abuf.at[c], recv_a.at[c]).start()
+    for fetch in fetches:
+        fetch.start()
+
+    @pl.when(c + place > 0)
+    def _():
+        pl.semaphore_wait(barrier, c + place)
 
     def copy_a(ch):
         return pltpu.make_async_remote_copy(
             src_ref=block_of(ch),
             dst_ref=abuf.at[c],
-            send_sem=send_a.at[ch],
+            send_sem=send_a,
             recv_sem=recv_a.at[c],
             device_id={"ch": ch},
             device_id_type=MESH,
         )
 
-    def offset(k):
-        return lax.rem(STRIDE * (k + s), n_ch)
-
-    @pl.loop(0, n_ch)
-    def _(k):
-        ch = lax.rem(c + offset(k), n_ch)
-
-        @pl.when(ch != c)
+    z, x = c // INNER, c % INNER
+    offsets = [(dz, dx) for dz in near_first(n_z) for dx in range(INNER)][1:]
+    for dz, dx in offsets:
+        ch = (z + dz + n_z) % n_z * INNER + (x + dx) % INNER
+
+        @pl.when(ch < c)
         def _():
             copy_a(ch).start()
 
-        @pl.when(ch == c)
-        def _():
-            pltpu.make_async_copy(block_of(c), abuf.at[c], recv_a.at[c]).start()
-
+    @pl.loop(0, c)
+    def _(ch):
+        pl.semaphore_signal(ready_a.at[c], inc=1, device_id={"ch": ch}, device_id_type=MESH)
+
+    @pl.loop(0, place)
+    def _(p):
+        pl.semaphore_signal(ready_b.at[s], inc=1, device_id={"ctx": ctx_at(p)}, device_id_type=MESH)
+
+    for fetch in fetches:
+        fetch.wait()
     col = lax.broadcasted_iota(jnp.int32, (recs, seq), 1)
     row = lax.broadcasted_iota(jnp.int32, (recs, seq), 0)
     pick = (row == (col // block) % group * n_ctx + s).astype(f32)
@@ -121,45 +155,73 @@
 
     met[0:MESSAGE, :] = jnp.zeros((MESSAGE, LANES), f32)
 
-    def landing(source, half):
-        return bbuf.at[source * group + half]
-
-    def copy_b(r):
-        return pltpu.make_async_remote_copy(
-            src_ref=abuf.at[r],
-            dst_ref=landing(s, r // n_ctx),
-            send_sem=send_b.at[r],
-            recv_sem=recv_b.at[s * group + r // n_ctx],
-            device_id={"ctx": lax.rem(r, n_ctx)},
-            device_id_type=MESH,
-        )
-
-    @pl.loop(0, n_ch)
-    def _(k):
-        r = lax.rem(c + n_ch - offset(k), n_ch)
+    chunk_id = lax.broadcasted_iota(jnp.int32, (CHUNKS, LANES), 0)
+
+    def spread_row(table, m):
+        return jnp.broadcast_to(table[m : m + 1, :], (CHUNKS, LANES))
+
+    rate = rate_ref[...]
+    gain = res_ref[...] * jnp.sqrt(2.0 * rate / modes)
+    grow = jnp.exp(rate)
+    hops = (1, 2, 4)
+    named = [jnp.exp(-rate), gain, grow, gain * grow, jnp.exp(-rate * (seq - 1)), jnp.exp(-rate * (seq - 2))]
+    named += [jnp.exp(-rate * (steps * hop)) for hop in hops]
+    for shard in range(n_ctx - 1):
+        behind = s - 1 - shard
+        reach = jnp.exp(-rate * (seq * jnp.maximum(behind, 0)).astype(f32))
+        named.append(jnp.where(behind >= 0, reach, 0.0))
+    for i, table in enumerate(named):
+        tables[i] = table
+    since = (chunk_id * steps + 1).astype(f32)
+    for m in range(modes):
+        starts[m] = spread_row(gain, m) * jnp.exp(-spread_row(rate, m) * since)
+
+    @pl.loop(c + 1, n_ch)
+    def _(ch):
+        pl.semaphore_wait(ready_a.at[ch], 1)
+        copy_a(ch).start()
+
+    @pl.loop(place + 1, n_ctx)
+    def _(p):
+        pl.semaphore_wait(ready_b.at[ctx_at(p)], 1)
+
+    def forward(r):
         pltpu.make_async_copy(abuf.at[r], abuf.at[r], recv_a.at[r]).wait()
-        owner = lax.rem(r, n_ctx)
+        owner, here = r % n_ctx, s * group + r // n_ctx
 
         @pl.when(owner != s)
         def _():
-            copy_b(r).start()
+            pltpu.make_async_remote_copy(
+                src_ref=abuf.at[r],
+                dst_ref=bbuf.at[here],
+                send_sem=send_b,
+                recv_sem=recv_b,
+                device_id={"ctx": owner},
+                device_id_type=MESH,
+            ).start()
 
         @pl.when(owner == s)
         def _():
-            i = s * group + r // n_ctx
-            pltpu.make_async_copy(abuf.at[r], bbuf.at[i], recv_b.at[i]).start()
-
-    rate = rate_ref[...]
-    decay = jnp.exp(-rate)
-    gain = res_ref[...] * jnp.sqrt(2.0 * rate / modes)
-    chunk_id = lax.broadcasted_iota(jnp.int32, (CHUNKS, LANES), 0)
-
-    def spread_row(table, m):
-        return jnp.broadcast_to(table[m : m + 1, :], (CHUNKS, LANES))
-
-    @pl.loop(0, n_ch)
-    def _(i):
-        pltpu.make_async_copy(bbuf.at[i], bbuf.at[i], recv_b.at[i]).wait()
+            pltpu.make_async_copy(abuf.at[r], bbuf.at[here], recv_b).start()
+
+    for dz, dx in offsets:
+        r = (z - dz + n_z) % n_z * INNER + (x - dx + INNER) % INNER
+
+        @pl.when(r < c)
+        def _():
+            forward(r)
+
+    @pl.loop(c, n_ch)
+    def _(r):
+        forward(r)
+
+    pltpu.make_async_copy(bbuf, bbuf, recv_b).wait()
+
+    def table(i):
+        return tables[i]
+
+    def table_row(i, m):
+        return jnp.broadcast_to(tables[i, m : m + 1, :], (CHUNKS, LANES))
 
     for j in range(3):
         placed[j] = jnp.dot(
@@ -167,7 +229,7 @@
         )
 
     taps = [[jnp.broadcast_to(w_ref[j, i : i + 1, :], (CHUNKS, LANES)) for i in range(3)] for j in range(3)]
-    decays = [spread_row(decay, m) for m in range(modes)]
+    decays = [table_row(0, m) for m in range(modes)]
     before = [
         [
             jnp.where(chunk_id == 0, 0.0, pltpu.roll(placed[j, (steps - i) * CHUNKS : (steps - i + 1) * CHUNKS, :], 1, 0))
@@ -197,9 +259,8 @@
     start = []
     for m in range(modes):
         total = state[m]
-        for hop in (1, 2, 4):
-            power = spread_row(jnp.exp(-rate[m : m + 1, :] * (steps * hop)), 0)
-            total = total + power * jnp.where(chunk_id >= hop, pltpu.roll(total, hop, 0), 0.0)
+        for i, hop in enumerate(hops):
+            total = total + table_row(6 + i, m) * jnp.where(chunk_id >= hop, pltpu.roll(total, hop, 0), 0.0)
         local[m : m + 1, :] = total[CHUNKS - 1 :, :]
         start.append(jnp.where(chunk_id >= 1, pltpu.roll(total, 1, 0), 0.0))
     for j in range(3):
@@ -228,7 +289,7 @@
 
     met[pl.ds(pl.multiple_of((s + 1) * MESSAGE, MESSAGE), MESSAGE), :] = local[...]
 
-    gains = [spread_row(gain, m) for m in range(modes)]
+    gains = [table_row(1, m) for m in range(modes)]
 
     def second_pass(t, state):
         at = pl.ds(pl.multiple_of(t * CHUNKS, CHUNKS), CHUNKS)
@@ -263,19 +324,13 @@
     here = met[pl.ds(pl.multiple_of(s * MESSAGE, MESSAGE), 2 * MESSAGE), :]
     q0, p0, q1, p1 = rim_products(lambda i: here[i : i + 1, :])
 
-    back0 = jnp.exp(-rate * (seq - 1))
-    back1 = jnp.exp(-rate * (seq - 2))
     entering = jnp.zeros((modes, LANES), f32)
     for shard in range(n_ctx - 1):
-        behind = s - 1 - shard
-        reach = jnp.exp(-rate * (seq * jnp.maximum(behind, 0)).astype(f32))
-        reach = jnp.where(behind >= 0, reach, 0.0)
         ended = met[(shard + 1) * MESSAGE : (shard + 1) * MESSAGE + modes, :]
-        ended = ended + back0 * all0[shard : shard + 1, :] + back1 * all1[shard : shard + 1, :]
-        entering = entering + reach * ended
-    grow = jnp.exp(rate)
-    entering = entering + grow * (p0 + grow * p1)
-    early = jnp.sum(gain * grow, axis=0, keepdims=True) * p1
+        ended = ended + table(4) * all0[shard : shard + 1, :] + table(5) * all1[shard : shard + 1, :]
+        entering = entering + table(9 + shard) * ended
+    entering = entering + table(2) * (p0 + table(2) * p1)
+    early = jnp.sum(table(3), axis=0, keepdims=True) * p1
 
     pbuf[0:1, :] = p0
     qbuf[0:1, :] = q0
@@ -283,10 +338,7 @@
     qbuf[CHUNKS : CHUNKS + 1, :] = q1
     ybuf[0:1, :] = ybuf[0:1, :] - early
 
-    since = (chunk_id * steps + 1).astype(f32)
-    coming = [
-        spread_row(gain * entering, m) * jnp.exp(-spread_row(rate, m) * since) for m in range(modes)
-    ]
+    coming = [starts[m] * spread_row(entering, m) for m in range(modes)]
     direct = jnp.broadcast_to(pass_ref[...], (CHUNKS, LANES))
 
     def third_pass(t, coming):
@@ -301,15 +353,8 @@
     lax.fori_loop(0, steps, third_pass, coming, unroll=2)
     out_ref[...] = tail[...].astype(out_ref.dtype)
 
-    @pl.loop(1, n_ch)
-    def _(k):
-        copy_a(lax.rem(c + k, n_ch)).wait_send()
-
-    @pl.loop(0, n_ch)
-    def _(r):
-        @pl.when(lax.rem(r, n_ctx) != s)
-        def _():
-            copy_b(r).wait_send()
+    pltpu.make_async_copy(abuf.at[1:], abuf.at[1:], send_a).wait()
+    pltpu.make_async_copy(abuf.at[group:], abuf.at[group:], send_b).wait()
 
     @pl.loop(s + 1, n_ctx)
     def _(shard):
@@ -326,9 +371,14 @@
     return pl.pallas_call(
         functools.partial(kernel, n_ctx, n_ch, block, modes),
         out_shape=jax.ShapeDtypeStruct((seq, LANES), jnp.bfloat16),
-        in_specs=[pl.BlockSpec(memory_space=pl.ANY)] + [vmem] * 5,
+        in_specs=[pl.BlockSpec(memory_space=pl.ANY)] * 6,
         out_specs=vmem,
         scratch_shapes=[
+            pltpu.VMEM(rec_slot.shape, jnp.int32),
+            pltpu.VMEM((3, 3, LANES), f32),
+            pltpu.VMEM((modes, LANES), f32),
+            pltpu.VMEM((modes, LANES), f32),
+            pltpu.VMEM((1, LANES), f32),
             pltpu.VMEM((n_ch, 3, block, LANES), jnp.bfloat16),
             pltpu.VMEM((n_ch, 3, block, LANES), jnp.bfloat16),
             pltpu.VMEM((seq, seq), jnp.bfloat16),
@@ -339,15 +389,20 @@
             pltpu.VMEM((seq, LANES), f32),
             pltpu.VMEM((MESSAGE, LANES), f32),
             pltpu.VMEM(((n_ctx + 1) * MESSAGE, LANES), f32),
+            pltpu.VMEM((8 + n_ctx, modes, LANES), f32),
+            pltpu.VMEM((modes, CHUNKS, LANES), f32),
+            dma((5,)),
+            dma,
             dma((n_ch,)),
-            dma((n_ch,)),
-            dma((n_ch,)),
-            dma((n_ch,)),
+            dma,
+            dma,
             dma((n_ctx,)),
             dma((n_ctx,)),
+            pltpu.SemaphoreType.REGULAR((n_ch,)),
+            pltpu.SemaphoreType.REGULAR((n_ctx,)),
         ],
         compiler_params=pltpu.CompilerParams(
-            collective_id=0, has_side_effects=True, vmem_limit_bytes=48 * 1024 * 1024
+            collective_id=0, has_side_effects=True, vmem_limit_bytes=61 * 1024 * 1024
         ),
         name="hyena",
     )(

time: 47.8 us -> 42.4 us (0.89)
  the two profiles are of different devices: /device:TPU:48 before, /device:TPU:497 now
where the time goes in v2:
time: 42.4 us; the launch traced here: 42.2 us
  Pallas kernels  40.6 us (96%)
  local copies, waits for them, and re-layouts  1.57 us (4%)
    pallas_call x1, Pallas kernels, shards(): pl.pallas_call(functools.partial(kernel, n_ctx, n_ch, block, modes), out_...  40.6 us
    unnamed x1, local copies, waits for them, and re-layouts  1.57 us

profile of v2, /device:TPU:497, one launch (start us, length us, event | category | flops | bytes accessed | tf_op | source)
XLA Modules:
  0.0 42.2 jit_solution(2701605840248518145)
XLA Ops:
  0.0 40.6 %hyena.1 = bf16[512,128]{1,0:T(8,128)(2,1)} custom-call(bf16[3,16,4096]{2,1,0:T(8,128)(2,1)} %bitcast.5, s32[16,32]{1,0:T(8,128)} %slot_hbm.1, f32[3,3,128]{2,1,0:T(4,128)} %bitcast.8, f32[16,128]{1,0:T(8,128)} %bitcast.6, f32[16,128]{1,0:T(8,128)} %bitcast.7, f32[1,128]{1,0:T(1,128)} %bitcast.9), custom_call_target="tpu_custom_call" | custom-call | tf_op jit(solution)/shard_map/hyena/pallas_call | solution.py:371
  40.6 1.6 %copy.8 = bf16[512,128]{1,0:T(8,128)(2,1)} copy(bf16[512,128]{1,0:T(8,128)(2,1)} %hyena.1) | data formatting | bytes 262144

commit v3 on v2

--- a/solution.py
+++ b/solution.py
@@ -45,7 +45,9 @@
     ybuf,
     tail,
     local,
+    sent,
     met,
+    got,
     tables,
     starts,
     load,
@@ -151,9 +153,9 @@
 
     @pl.loop(s + 2, n_ctx + 1)
     def _(i):
-        met[pl.ds(pl.multiple_of(i * MESSAGE, MESSAGE), MESSAGE), :] = jnp.zeros((MESSAGE, LANES), f32)
-
-    met[0:MESSAGE, :] = jnp.zeros((MESSAGE, LANES), f32)
+        met[pl.ds(pl.multiple_of(i * MESSAGE, MESSAGE), MESSAGE), :] = jnp.zeros((MESSAGE, LANES), jnp.bfloat16)
+
+    met[0:MESSAGE, :] = jnp.zeros((MESSAGE, LANES), jnp.bfloat16)
 
     chunk_id = lax.broadcasted_iota(jnp.int32, (CHUNKS, LANES), 0)
 
@@ -269,13 +271,14 @@
             at = (steps - 2 + i) * CHUNKS + CHUNKS - 1
             local[modes + 6 + 2 * j + i : modes + 7 + 2 * j + i, :] = placed[j, at : at + 1, :]
     local[modes + 12 :, :] = jnp.zeros((MESSAGE - modes - 12, LANES), f32)
+    sent[...] = local[...].astype(jnp.bfloat16)
 
     def slab(shard):
         return met.at[pl.ds(pl.multiple_of((shard + 1) * MESSAGE, MESSAGE), MESSAGE)]
 
     def copy_c(shard):
         return pltpu.make_async_remote_copy(
-            src_ref=local,
+            src_ref=sent,
             dst_ref=slab(s),
             send_sem=send_c.at[shard],
             recv_sem=recv_c.at[s],
@@ -287,7 +290,7 @@
     def _(shard):
         copy_c(shard).start()
 
-    met[pl.ds(pl.multiple_of((s + 1) * MESSAGE, MESSAGE), MESSAGE), :] = local[...]
+    met[pl.ds(pl.multiple_of((s + 1) * MESSAGE, MESSAGE), MESSAGE), :] = sent[...]
 
     gains = [table_row(1, m) for m in range(modes)]
 
@@ -307,8 +310,7 @@
     def _(shard):
         pltpu.make_async_copy(slab(shard), slab(shard), recv_c.at[shard]).wait()
 
-    def rim(row, width, base, stride):
-        return met[pl.ds(base + row, width, stride=stride), :]
+    got[...] = met[...].astype(f32)
 
     def rim_products(pick_row):
         first, second = [], []
@@ -320,13 +322,13 @@
             second.append(tap[0] * x1 + tap[1] * x0 + tap[2] * l1)
         return first[0], first[1] * first[2], second[0], second[1] * second[2]
 
-    _, all0, _, all1 = rim_products(lambda i: met[pl.ds(i, n_ctx, stride=MESSAGE), :])
-    here = met[pl.ds(pl.multiple_of(s * MESSAGE, MESSAGE), 2 * MESSAGE), :]
+    _, all0, _, all1 = rim_products(lambda i: got[pl.ds(i, n_ctx, stride=MESSAGE), :])
+    here = got[pl.ds(pl.multiple_of(s * MESSAGE, MESSAGE), 2 * MESSAGE), :]
     q0, p0, q1, p1 = rim_products(lambda i: here[i : i + 1, :])
 
     entering = jnp.zeros((modes, LANES), f32)
     for shard in range(n_ctx - 1):
-        ended = met[(shard + 1) * MESSAGE : (shard + 1) * MESSAGE + modes, :]
+        ended = got[(shard + 1) * MESSAGE : (shard + 1) * MESSAGE + modes, :]
         ended = ended + table(4) * all0[shard : shard + 1, :] + table(5) * all1[shard : shard + 1, :]
         entering = entering + table(9 + shard) * ended
     entering = entering + table(2) * (p0 + table(2) * p1)
@@ -370,7 +372,7 @@
     dma = pltpu.SemaphoreType.DMA
     return pl.pallas_call(
         functools.partial(kernel, n_ctx, n_ch, block, modes),
-        out_shape=jax.ShapeDtypeStruct((seq, LANES), jnp.bfloat16),
+        out_shape=pltpu.VMEM((seq, LANES), jnp.bfloat16),
         in_specs=[pl.BlockSpec(memory_space=pl.ANY)] * 6,
         out_specs=vmem,
         scratch_shapes=[
@@ -388,6 +390,8 @@
             pltpu.VMEM((seq, LANES), f32),
             pltpu.VMEM((seq, LANES), f32),
             pltpu.VMEM((MESSAGE, LANES), f32),
+            pltpu.VMEM((MESSAGE, LANES), jnp.bfloat16),
+            pltpu.VMEM(((n_ctx + 1) * MESSAGE, LANES), jnp.bfloat16),
             pltpu.VMEM(((n_ctx + 1) * MESSAGE, LANES), f32),
             pltpu.VMEM((8 + n_ctx, modes, LANES), f32),
             pltpu.VMEM((modes, CHUNKS, LANES), f32),

time: 42.4 us -> 38.1 us (0.90)
  Pallas kernels: 40.6 us -> 37.3 us
  local copies, waits for them, and re-layouts: 1.57 us -> 0.66 us
    pallas_call x1, Pallas kernels: 40.6 us -> 37.3 us  [shards(): pl.pallas_call(functools.partial(kernel, n_ctx, n_ch, block, modes), out_...]
    unnamed x1, local copies, waits for them, and re-layouts: 1.57 us -> 0.66 us
where the time goes in v3:
time: 38.1 us; the launch traced here: 38 us
  Pallas kernels  37.3 us (98%)
  local copies, waits for them, and re-layouts  0.66 us (2%)
    pallas_call x1, Pallas kernels, shards(): pl.pallas_call(functools.partial(kernel, n_ctx, n_ch, block, modes), out_...  37.3 us

profile of v3, /device:TPU:497, one launch (start us, length us, event | category | flops | bytes accessed | tf_op | source)
XLA Modules:
  0.0 38.0 jit_solution(7480280705393394283)
XLA Ops:
  0.0 37.3 %hyena.1 = bf16[512,128]{1,0:T(8,128)(2,1)S(1)} custom-call(bf16[3,16,4096]{2,1,0:T(8,128)(2,1)} %bitcast.5, s32[16,32]{1,0:T(8,128)} %slot_hbm.1, f32[3,3,128]{2,1,0:T(4,128)} %bitcast.8, f32[16,128]{1,0:T(8,128)} %bitcast.6, f32[16,128]{1,0:T(8,128)} %bitcast.7, f32[1,128]{1,0:T(1,128)} %bitcast.9), custom_call_target="tpu_custom_call" | custom-call | tf_op jit(solution)/shard_map/hyena/pallas_call | solution.py:373
  37.3 0.7 %copy.8 = bf16[512,128]{1,0:T(8,128)(2,1)} copy(bf16[512,128]{1,0:T(8,128)(2,1)S(1)} %hyena.1) | data formatting | bytes 262144

commit v4 on v3

--- a/solution.py
+++ b/solution.py
@@ -31,6 +31,7 @@
     rate_hbm,
     pass_hbm,
     out_ref,
+    x_ref,
     slot_ref,
     w_ref,
     res_ref,
@@ -92,10 +93,12 @@
     def _(p):
         pl.semaphore_signal(barrier, inc=1, device_id={"ctx": ctx_at(p)}, device_id_type=MESH)
 
-    def block_of(ch):
-        return x_hbm.at[:, :, pl.ds(pl.multiple_of(ch * LANES, LANES), LANES)]
+    def block_of(ch, source=x_hbm):
+        return source.at[:, :, pl.ds(pl.multiple_of(ch * LANES, LANES), LANES)]
 
     pltpu.make_async_copy(block_of(c), abuf.at[c], recv_a.at[c]).start()
+    x_copy = pltpu.make_async_copy(x_hbm, x_ref, load.at[5])
+    x_copy.start()
     for fetch in fetches:
         fetch.start()
 
@@ -103,9 +106,9 @@
     def _():
         pl.semaphore_wait(barrier, c + place)
 
-    def copy_a(ch):
+    def copy_a(ch, source=x_hbm):
         return pltpu.make_async_remote_copy(
-            src_ref=block_of(ch),
+            src_ref=block_of(ch, source),
             dst_ref=abuf.at[c],
             send_sem=send_a,
             recv_sem=recv_a.at[c],
@@ -115,20 +118,26 @@
 
     z, x = c // INNER, c % INNER
     offsets = [(dz, dx) for dz in near_first(n_z) for dx in range(INNER)][1:]
-    for dz, dx in offsets:
-        ch = (z + dz + n_z) % n_z * INNER + (x + dx) % INNER
+    for i in range(n_ch):
+        ch = i // INNER * INNER + (x + i) % INNER
 
         @pl.when(ch < c)
         def _():
+            pl.semaphore_signal(ready_a.at[c], inc=1, device_id={"ch": ch}, device_id_type=MESH)
             copy_a(ch).start()
-
-    @pl.loop(0, c)
-    def _(ch):
-        pl.semaphore_signal(ready_a.at[c], inc=1, device_id={"ch": ch}, device_id_type=MESH)
 
     @pl.loop(0, place)
     def _(p):
         pl.semaphore_signal(ready_b.at[s], inc=1, device_id={"ctx": ctx_at(p)}, device_id_type=MESH)
+
+    half = n_ch // 2
+
+    def send_later(ch):
+        pl.semaphore_wait(ready_a.at[ch], 1)
+        copy_a(ch, x_ref).start()
+
+    x_copy.wait()
+    pl.loop(c + 1, jnp.where(c < half, half, n_ch))(send_later)
 
     for fetch in fetches:
         fetch.wait()
@@ -178,14 +187,7 @@
     for m in range(modes):
         starts[m] = spread_row(gain, m) * jnp.exp(-spread_row(rate, m) * since)
 
-    @pl.loop(c + 1, n_ch)
-    def _(ch):
-        pl.semaphore_wait(ready_a.at[ch], 1)
-        copy_a(ch).start()
-
-    @pl.loop(place + 1, n_ctx)
-    def _(p):
-        pl.semaphore_wait(ready_b.at[ctx_at(p)], 1)
+    pl.loop(half, jnp.where(c < half, n_ch, half))(send_later)
 
     def forward(r):
         pltpu.make_async_copy(abuf.at[r], abuf.at[r], recv_a.at[r]).wait()
@@ -206,16 +208,48 @@
         def _():
             pltpu.make_async_copy(abuf.at[r], bbuf.at[here], recv_b).start()
 
-    for dz, dx in offsets:
-        r = (z - dz + n_z) % n_z * INNER + (x - dx + INNER) % INNER
-
-        @pl.when(r < c)
+    def first(r):
+        @pl.when(place_of(r) > place)
         def _():
+            pl.semaphore_wait(ready_b.at[r], 1)
+
+        forward(r)
+
+    @pl.when(c < n_ch // 2)
+    def _():
+        for dz, dx in offsets:
+            r = (z - dz + n_z) % n_z * INNER + (x - dx + INNER) % INNER
+
+            @pl.when((r < c) & (r < n_ctx))
+            def _():
+                first(r)
+
+        @pl.loop(c, n_ctx)
+        def _(r):
+            first(r)
+
+        for dz, dx in offsets:
+            r = (z - dz + n_z) % n_z * INNER + (x - dx + INNER) % INNER
+
+            @pl.when((r < c) & (r >= n_ctx))
+            def _():
+                forward(r)
+
+        @pl.loop(jnp.maximum(c, n_ctx), n_ch)
+        def _(r):
             forward(r)
 
-    @pl.loop(c, n_ch)
-    def _(r):
-        forward(r)
+
+    @pl.when(c >= n_ch // 2)
+    def _():
+        @pl.loop(0, n_ctx)
+        def _(k):
+            first((s + n_ctx - 1 - k) % n_ctx)
+
+        @pl.loop(0, n_ctx)
+        def _(k):
+            forward((s + n_ctx - 1 - k) % n_ctx + n_ctx)
+
 
     pltpu.make_async_copy(bbuf, bbuf, recv_b).wait()
 
@@ -376,6 +410,7 @@
         in_specs=[pl.BlockSpec(memory_space=pl.ANY)] * 6,
         out_specs=vmem,
         scratch_shapes=[
+            pltpu.VMEM((3, block, channels), jnp.bfloat16),
             pltpu.VMEM(rec_slot.shape, jnp.int32),
             pltpu.VMEM((3, 3, LANES), f32),
             pltpu.VMEM((modes, LANES), f32),
@@ -395,7 +430,7 @@
             pltpu.VMEM(((n_ctx + 1) * MESSAGE, LANES), f32),
             pltpu.VMEM((8 + n_ctx, modes, LANES), f32),
             pltpu.VMEM((modes, CHUNKS, LANES), f32),
-            dma((5,)),
+            dma((6,)),
             dma,
             dma((n_ch,)),
             dma,

time: 38.1 us -> 36.9 us (0.969)
  the two profiles are of different devices: /device:TPU:497 before, /device:TPU:441 now
where the time goes in v4:
time: 36.9 us; the launch traced here: 36.8 us
  Pallas kernels  36.1 us (98%)
  local copies, waits for them, and re-layouts  0.66 us (2%)
    pallas_call x1, Pallas kernels, shards(): pl.pallas_call(functools.partial(kernel, n_ctx, n_ch, block, modes), out_...  36.1 us

profile of v4, /device:TPU:441, one launch (start us, length us, event | category | flops | bytes accessed | tf_op | source)
XLA Modules:
  0.0 36.8 jit_solution(9381416071415312963)
XLA Ops:
  0.0 36.1 %hyena.1 = bf16[512,128]{1,0:T(8,128)(2,1)S(1)} custom-call(bf16[3,16,4096]{2,1,0:T(8,128)(2,1)} %bitcast.5, s32[16,32]{1,0:T(8,128)} %slot_hbm.1, f32[3,3,128]{2,1,0:T(4,128)} %bitcast.8, f32[16,128]{1,0:T(8,128)} %bitcast.6, f32[16,128]{1,0:T(8,128)} %bitcast.7, f32[1,128]{1,0:T(1,128)} %bitcast.9), custom_call_target="tpu_custom_call" | custom-call | tf_op jit(solution)/shard_map/hyena/pallas_call | solution.py:407
  36.1 0.7 %copy.8 = bf16[512,128]{1,0:T(8,128)(2,1)} copy(bf16[512,128]{1,0:T(8,128)(2,1)S(1)} %hyena.1) | data formatting | bytes 262144

commit v5 on v4

--- a/solution.py
+++ b/solution.py
@@ -17,6 +17,14 @@
 
 def near_first(count):
     return [(i + 1) // 2 if i % 2 else -(i // 2) for i in range(count)]
+
+
+def rest(value, count):
+    return value & (count - 1)
+
+
+def times(value, count):
+    return value >> (count.bit_length() - 1)
 
 
 def kernel(
@@ -71,12 +79,12 @@
     n_z, n_y = n_ch // INNER, n_ctx // CORES
 
     def place_of(ctx):
-        y = ctx // CORES
-        return jnp.where(y == 0, 0, jnp.where(y <= n_y // 2, 2 * y - 1, 2 * (n_y - y))) * CORES + ctx % CORES
+        y = times(ctx, CORES)
+        return jnp.where(y == 0, 0, jnp.where(y <= n_y // 2, 2 * y - 1, 2 * (n_y - y))) * CORES + rest(ctx, CORES)
 
     def ctx_at(place):
-        i = place // CORES
-        return jnp.where(i == 0, 0, jnp.where(i % 2 == 1, (i + 1) // 2, n_y - i // 2)) * CORES + place % CORES
+        i = times(place, CORES)
+        return jnp.where(rest(i, 2) == 1, times(i + 1, 2), rest(n_y - times(i, 2), n_y)) * CORES + rest(place, CORES)
 
     place = place_of(s)
 
@@ -116,10 +124,10 @@
             device_id_type=MESH,
         )
 
-    z, x = c // INNER, c % INNER
+    z, x = times(c, INNER), rest(c, INNER)
     offsets = [(dz, dx) for dz in near_first(n_z) for dx in range(INNER)][1:]
     for i in range(n_ch):
-        ch = i // INNER * INNER + (x + i) % INNER
+        ch = i // INNER * INNER + rest(x + i, INNER)
 
         @pl.when(ch < c)
         def _():
@@ -191,7 +199,7 @@
 
     def forward(r):
         pltpu.make_async_copy(abuf.at[r], abuf.at[r], recv_a.at[r]).wait()
-        owner, here = r % n_ctx, s * group + r // n_ctx
+        owner, here = rest(r, n_ctx), s * group + times(r, n_ctx)
 
         @pl.when(owner != s)
         def _():
@@ -218,7 +226,7 @@
     @pl.when(c < n_ch // 2)
     def _():
         for dz, dx in offsets:
-            r = (z - dz + n_z) % n_z * INNER + (x - dx + INNER) % INNER
+            r = rest(z - dz, n_z) * INNER + rest(x - dx, INNER)
 
             @pl.when((r < c) & (r < n_ctx))
             def _():
@@ -229,7 +237,7 @@
             first(r)
 
         for dz, dx in offsets:
-            r = (z - dz + n_z) % n_z * INNER + (x - dx + INNER) % INNER
+            r = rest(z - dz, n_z) * INNER + rest(x - dx, INNER)
 
             @pl.when((r < c) & (r >= n_ctx))
             def _():
@@ -244,11 +252,11 @@
     def _():
         @pl.loop(0, n_ctx)
         def _(k):
-            first((s + n_ctx - 1 - k) % n_ctx)
+            first(rest(s + n_ctx - 1 - k, n_ctx))
 
         @pl.loop(0, n_ctx)
         def _(k):
-            forward((s + n_ctx - 1 - k) % n_ctx + n_ctx)
+            forward(rest(s + n_ctx - 1 - k, n_ctx) + n_ctx)
 
 
     pltpu.make_async_copy(bbuf, bbuf, recv_b).wait()
@@ -259,16 +267,17 @@
     def table_row(i, m):
         return jnp.broadcast_to(tables[i, m : m + 1, :], (CHUNKS, LANES))
 
-    for j in range(3):
-        placed[j] = jnp.dot(
-            perm[...], bbuf[:, j].reshape(seq, LANES), preferred_element_type=f32
-        )
+    arrived = jnp.concatenate([bbuf[:, j].reshape(seq, LANES) for j in range(3)], axis=1)
+    placed[...] = jnp.dot(perm[...], arrived, preferred_element_type=f32)
+
+    def stream(j, start):
+        return placed[pl.ds(start, CHUNKS), j * LANES : (j + 1) * LANES]
 
     taps = [[jnp.broadcast_to(w_ref[j, i : i + 1, :], (CHUNKS, LANES)) for i in range(3)] for j in range(3)]
     decays = [table_row(0, m) for m in range(modes)]
     before = [
         [
-            jnp.where(chunk_id == 0, 0.0, pltpu.roll(placed[j, (steps - i) * CHUNKS : (steps - i + 1) * CHUNKS, :], 1, 0))
+            jnp.where(chunk_id == 0, 0.0, pltpu.roll(stream(j, (steps - i) * CHUNKS), 1, 0))
             for j in range(3)
         ]
         for i in (1, 2)
@@ -277,7 +286,7 @@
     def first_pass(t, carry):
         one, two, state = carry
         at = pl.ds(pl.multiple_of(t * CHUNKS, CHUNKS), CHUNKS)
-        now = [placed[j, at, :] for j in range(3)]
+        now = [stream(j, pl.multiple_of(t * CHUNKS, CHUNKS)) for j in range(3)]
         feats = [taps[j][0] * now[j] + taps[j][1] * one[j] + taps[j][2] * two[j] for j in range(3)]
         product = feats[1] * feats[2]
         if isinstance(t, int):
@@ -301,9 +310,9 @@
         start.append(jnp.where(chunk_id >= 1, pltpu.roll(total, 1, 0), 0.0))
     for j in range(3):
         for i in range(2):
-            local[modes + 2 * j + i : modes + 2 * j + i + 1, :] = placed[j, i * CHUNKS : i * CHUNKS + 1, :]
+            local[modes + 2 * j + i : modes + 2 * j + i + 1, :] = placed[i * CHUNKS : i * CHUNKS + 1, j * LANES : (j + 1) * LANES]
             at = (steps - 2 + i) * CHUNKS + CHUNKS - 1
-            local[modes + 6 + 2 * j + i : modes + 7 + 2 * j + i, :] = placed[j, at : at + 1, :]
+            local[modes + 6 + 2 * j + i : modes + 7 + 2 * j + i, :] = placed[at : at + 1, j * LANES : (j + 1) * LANES]
     local[modes + 12 :, :] = jnp.zeros((MESSAGE - modes - 12, LANES), f32)
     sent[...] = local[...].astype(jnp.bfloat16)
 
@@ -321,8 +330,8 @@
         )
 
     @pl.loop(s + 1, n_ctx)
-    def _(shard):
-        copy_c(shard).start()
+    def _(i):
+        copy_c(s + n_ctx - i).start()
 
     met[pl.ds(pl.multiple_of((s + 1) * MESSAGE, MESSAGE), MESSAGE), :] = sent[...]
 
@@ -419,7 +428,7 @@
             pltpu.VMEM((n_ch, 3, block, LANES), jnp.bfloat16),
             pltpu.VMEM((n_ch, 3, block, LANES), jnp.bfloat16),
             pltpu.VMEM((seq, seq), jnp.bfloat16),
-            pltpu.VMEM((3, seq, LANES), f32),
+            pltpu.VMEM((seq, 3 * LANES), f32),
             pltpu.VMEM((seq, LANES), f32),
             pltpu.VMEM((seq, LANES), f32),
             pltpu.VMEM((seq, LANES), f32),

time: 36.9 us -> 36.5 us (0.989)
  the two profiles are of different devices: /device:TPU:441 before, /device:TPU:440 now
where the time goes in v5:
time: 36.5 us; the launch traced here: 36.3 us
  Pallas kernels  35.7 us (98%)
  local copies, waits for them, and re-layouts  0.66 us (2%)
    pallas_call x1, Pallas kernels, shards(): pl.pallas_call(functools.partial(kernel, n_ctx, n_ch, block, modes), out_...  35.7 us

profile of v5, /device:TPU:440, one launch (start us, length us, event | category | flops | bytes accessed | tf_op | source)
XLA Modules:
  0.0 36.3 jit_solution(9280919830734511211)
XLA Ops:
  0.0 35.7 %hyena.1 = bf16[512,128]{1,0:T(8,128)(2,1)S(1)} custom-call(bf16[3,16,4096]{2,1,0:T(8,128)(2,1)} %bitcast.5, s32[16,32]{1,0:T(8,128)} %slot_hbm.1, f32[3,3,128]{2,1,0:T(4,128)} %bitcast.8, f32[16,128]{1,0:T(8,128)} %bitcast.6, f32[16,128]{1,0:T(8,128)} %bitcast.7, f32[1,128]{1,0:T(1,128)} %bitcast.9), custom_call_target="tpu_custom_call" | custom-call | tf_op jit(solution)/shard_map/hyena/pallas_call | solution.py:416
  35.7 0.7 %copy.8 = bf16[512,128]{1,0:T(8,128)(2,1)} copy(bf16[512,128]{1,0:T(8,128)(2,1)S(1)} %hyena.1) | data formatting | bytes 262144

commit v6 on v5

--- a/solution.py
+++ b/solution.py
@@ -217,46 +217,34 @@
             pltpu.make_async_copy(abuf.at[r], bbuf.at[here], recv_b).start()
 
     def first(r):
-        @pl.when(place_of(r) > place)
+        owner = rest(r, n_ctx)
+
+        @pl.when(place_of(owner) > place)
         def _():
-            pl.semaphore_wait(ready_b.at[r], 1)
+            pl.semaphore_wait(ready_b.at[owner], 1)
 
         forward(r)
 
     @pl.when(c < n_ch // 2)
     def _():
-        for dz, dx in offsets:
-            r = rest(z - dz, n_z) * INNER + rest(x - dx, INNER)
-
-            @pl.when((r < c) & (r < n_ctx))
-            def _():
-                first(r)
-
-        @pl.loop(c, n_ctx)
-        def _(r):
-            first(r)
-
-        for dz, dx in offsets:
-            r = rest(z - dz, n_z) * INNER + rest(x - dx, INNER)
-
-            @pl.when((r < c) & (r >= n_ctx))
-            def _():
-                forward(r)
-
-        @pl.loop(jnp.maximum(c, n_ctx), n_ch)
-        def _(r):
-            forward(r)
+        @pl.loop(0, n_ctx)
+        def _(k):
+            first(rest((z + times(k, INNER)) * INNER, n_ctx) + rest(k + s, INNER))
+
+        @pl.loop(0, n_ctx)
+        def _(k):
+            forward(n_ctx + (k & -INNER) + rest(k + times(s, CORES), INNER))
 
 
     @pl.when(c >= n_ch // 2)
     def _():
         @pl.loop(0, n_ctx)
         def _(k):
-            first(rest(s + n_ctx - 1 - k, n_ctx))
+            first(n_ctx + (k & -INNER) + rest(k + s, INNER))
 
         @pl.loop(0, n_ctx)
         def _(k):
-            forward(rest(s + n_ctx - 1 - k, n_ctx) + n_ctx)
+            forward(rest(s + n_ctx - 1 - k, n_ctx))
 
 
     pltpu.make_async_copy(bbuf, bbuf, recv_b).wait()

time: 36.5 us -> 34.7 us (0.951)
  the two profiles are of different devices: /device:TPU:440 before, /device:TPU:48 now
where the time goes in v6:
time: 34.7 us; the launch traced here: 34.6 us
  Pallas kernels  33.9 us (98%)
  local copies, waits for them, and re-layouts  0.66 us (2%)
    pallas_call x1, Pallas kernels, shards(): pl.pallas_call(functools.partial(kernel, n_ctx, n_ch, block, modes), out_...  33.9 us

profile of v6, /device:TPU:48, one launch (start us, length us, event | category | flops | bytes accessed | tf_op | source)
XLA Modules:
  0.0 34.6 jit_solution(5423690652271801062)
XLA Ops:
  0.0 33.9 %hyena.1 = bf16[512,128]{1,0:T(8,128)(2,1)S(1)} custom-call(bf16[3,16,4096]{2,1,0:T(8,128)(2,1)} %bitcast.5, s32[16,32]{1,0:T(8,128)} %slot_hbm.1, f32[3,3,128]{2,1,0:T(4,128)} %bitcast.8, f32[16,128]{1,0:T(8,128)} %bitcast.6, f32[16,128]{1,0:T(8,128)} %bitcast.7, f32[1,128]{1,0:T(1,128)} %bitcast.9), custom_call_target="tpu_custom_call" | custom-call | tf_op jit(solution)/shard_map/hyena/pallas_call | solution.py:404
  33.9 0.7 %copy.8 = bf16[512,128]{1,0:T(8,128)(2,1)} copy(bf16[512,128]{1,0:T(8,128)(2,1)S(1)} %hyena.1) | data formatting | bytes 262144

commit v7 on v6

--- a/solution.py
+++ b/solution.py
@@ -195,7 +195,7 @@
     for m in range(modes):
         starts[m] = spread_row(gain, m) * jnp.exp(-spread_row(rate, m) * since)
 
-    pl.loop(half, jnp.where(c < half, n_ch, half))(send_later)
+    pl.loop(half, jnp.where(c < half, half + 2 * INNER, half))(send_later)
 
     def forward(r):
         pltpu.make_async_copy(abuf.at[r], abuf.at[r], recv_a.at[r]).wait()
@@ -229,7 +229,9 @@
     def _():
         @pl.loop(0, n_ctx)
         def _(k):
-            first(rest((z + times(k, INNER)) * INNER, n_ctx) + rest(k + s, INNER))
+            first(rest((z + times(k, INNER)) * INNER, n_ctx) + rest(k + times(s, CORES), INNER))
+
+        pl.loop(half + 2 * INNER, n_ch)(send_later)
 
         @pl.loop(0, n_ctx)
         def _(k):

time: 34.7 us -> 34.4 us (level)
  no operation moved by 1% of the time
where the time goes in v7:
time: 34.4 us; the launch traced here: 34.3 us
  Pallas kernels  33.6 us (98%)
  local copies, waits for them, and re-layouts  0.66 us (2%)
    pallas_call x1, Pallas kernels, shards(): pl.pallas_call(functools.partial(kernel, n_ctx, n_ch, block, modes), out_...  33.6 us

profile of v7, /device:TPU:48, one launch (start us, length us, event | category | flops | bytes accessed | tf_op | source)
XLA Modules:
  0.0 34.3 jit_solution(4281597898971513044)
XLA Ops:
  0.0 33.6 %hyena.1 = bf16[512,128]{1,0:T(8,128)(2,1)S(1)} custom-call(bf16[3,16,4096]{2,1,0:T(8,128)(2,1)} %bitcast.5, s32[16,32]{1,0:T(8,128)} %slot_hbm.1, f32[3,3,128]{2,1,0:T(4,128)} %bitcast.8, f32[16,128]{1,0:T(8,128)} %bitcast.6, f32[16,128]{1,0:T(8,128)} %bitcast.7, f32[1,128]{1,0:T(1,128)} %bitcast.9), custom_call_target="tpu_custom_call" | custom-call | tf_op jit(solution)/shard_map/hyena/pallas_call | solution.py:406
  33.6 0.7 %copy.8 = bf16[512,128]{1,0:T(8,128)(2,1)} copy(bf16[512,128]{1,0:T(8,128)(2,1)S(1)} %hyena.1) | data formatting | bytes 262144

commit v8 on v7

--- a/solution.py
+++ b/solution.py
@@ -52,7 +52,6 @@
     pbuf,
     qbuf,
     ybuf,
-    tail,
     local,
     sent,
     met,
@@ -382,11 +381,10 @@
         while len(terms) > 1:
             terms = [a + b for a, b in zip(terms[::2], terms[1::2])]
         value = qbuf[at, :] * (ybuf[at, :] + terms[0] + direct * pbuf[at, :])
-        tail[pl.ds(t, CHUNKS, stride=steps), :] = value
+        out_ref[pl.ds(t, CHUNKS, stride=steps), :] = value
         return [decays[m] * coming[m] for m in range(modes)]
 
     lax.fori_loop(0, steps, third_pass, coming, unroll=2)
-    out_ref[...] = tail[...].astype(out_ref.dtype)
 
     pltpu.make_async_copy(abuf.at[1:], abuf.at[1:], send_a).wait()
     pltpu.make_async_copy(abuf.at[group:], abuf.at[group:], send_b).wait()
@@ -405,7 +403,7 @@
     dma = pltpu.SemaphoreType.DMA
     return pl.pallas_call(
         functools.partial(kernel, n_ctx, n_ch, block, modes),
-        out_shape=pltpu.VMEM((seq, LANES), jnp.bfloat16),
+        out_shape=pltpu.VMEM((seq, LANES), f32),
         in_specs=[pl.BlockSpec(memory_space=pl.ANY)] * 6,
         out_specs=vmem,
         scratch_shapes=[
@@ -419,7 +417,6 @@
             pltpu.VMEM((n_ch, 3, block, LANES), jnp.bfloat16),
             pltpu.VMEM((seq, seq), jnp.bfloat16),
             pltpu.VMEM((seq, 3 * LANES), f32),
-            pltpu.VMEM((seq, LANES), f32),
             pltpu.VMEM((seq, LANES), f32),
             pltpu.VMEM((seq, LANES), f32),
             pltpu.VMEM((seq, LANES), f32),
@@ -450,7 +447,7 @@
         residue.T,
         rate.T,
         passthrough[None, :],
-    )
+    ).astype(jnp.bfloat16)
 
 
 def solution(mesh):

time: 34.4 us -> 34.4 us (level)
  other arithmetic: 0 us -> 0.67 us
  local copies, waits for them, and re-layouts: 0.66 us -> 0 us
    convert_element_type x0 -> x1, other arithmetic: none -> 0.67 us  [shards(): return pl.pallas_call(functools.partial(kernel, n_ctx, n_ch, block, modes...]
    unnamed x1 -> x0, local copies, waits for them, and re-layouts: 0.66 us -> none
where the time goes in v8:
time: 34.4 us; the launch traced here: 34.3 us
  Pallas kernels  33.6 us (98%)
  other arithmetic  0.67 us (2%)
    pallas_call x1, Pallas kernels, shards(): pl.pallas_call(functools.partial(kernel, n_ctx, n_ch, block, modes), out_...  33.6 us

profile of v8, /device:TPU:48, one launch (start us, length us, event | category | flops | bytes accessed | tf_op | source)
XLA Modules:
  0.0 34.3 jit_solution(3300528218517250348)
XLA Ops:
  0.0 33.6 %hyena.1 = f32[512,128]{1,0:T(8,128)S(1)} custom-call(bf16[3,16,4096]{2,1,0:T(8,128)(2,1)} %bitcast.5, s32[16,32]{1,0:T(8,128)} %slot_hbm.1, f32[3,3,128]{2,1,0:T(4,128)} %bitcast.8, f32[16,128]{1,0:T(8,128)} %bitcast.6, f32[16,128]{1,0:T(8,128)} %bitcast.7, f32[1,128]{1,0:T(1,128)} %bitcast.9), custom_call_target="tpu_custom_call" | custom-call | tf_op jit(solution)/shard_map/hyena/pallas_call | solution.py:404
  33.6 0.7 %convert_element_type.3 = bf16[512,128]{1,0:T(8,128)(2,1)} convert(f32[512,128]{1,0:T(8,128)S(1)} %hyena.1) | non-fusion elementwise | flops 65536 | bytes 393216 | tf_op jit(solution)/shard_map/convert_element_type | solution.py:450
